TPU v7x, 512 devices: a whole 4x4x16 slice. The times are simulated.
512 devices in a mesh: dp: 2 (over core), seq: 16 (over y, x), head: 16 (over z).
Axes of the slice: x: 4, y: 4, z: 16, core: 2. Of those that a mesh axis runs over, the one named last changes fastest.
Arguments:
- queries: bfloat16 [65536, 32, 128], P(('dp', 'seq', 'head')), parts along dimension 0, may hold values from -6 to 6
- keys: bfloat16 [65536, 4, 128], P(('dp', 'seq', 'head')), parts along dimension 0, may hold values from -6 to 6
- values: bfloat16 [65536, 4, 128], P(('dp', 'seq', 'head')), parts along dimension 0, may hold values from -6 to 6
- out_grad: bfloat16 [65536, 32, 128], P(('dp', 'seq', 'head')), parts along dimension 0, may hold values from -24 to 24
- kept_blocks: int32 [4, 256, 1], replicated, may hold values from 0 to 255, as said below
- sink_blocks: int32 [4], replicated, may hold values from 1 to 3
- window_blocks: int32 [4], replicated, may hold values from 2 to 4
Outputs:
- grad_queries: bfloat16 [65536, 32, 128], P(('dp', 'seq', 'head')), parts along dimension 0
- grad_keys: bfloat16 [65536, 4, 128], P(('dp', 'seq', 'head')), parts along dimension 0
- grad_values: bfloat16 [65536, 4, 128], P(('dp', 'seq', 'head')), parts along dimension 0
There are 2 independent parts, one for each index of `dp`. A program takes and returns all parts, laid end to end along the dimension named above; an argument that names none is the same for every part. Nothing has to cross between parts.
Inputs may be any that keep to these rules, and one draw needn't show every extreme that they name: `kept_blocks`: entries that name a block after the query block are ignored; entries may name sink or window blocks. For each key head and each index of seq, the 16 entries of that index's query blocks name blocks held by one index of seq at most 2 times in all, and exactly 2 times for some index of seq.
All inputs are finite; a program needn't handle non-finite values.
Results may differ from a plain program's by a relative error of at most 0.0076.
Values may be sent and summed in bfloat16 or wider, within the bound.
A program may use at most 128 MiB of HBM per device.

v0:
```python
import math
import jax
import jax.numpy as jnp
import numpy as np
from jax import lax
from jax.sharding import PartitionSpec as P

BLK = 128
SINK_MOST = 3
WIN_MOST = 4


def spread(array, axis, root):
    mine = lax.axis_index(axis) == root
    return lax.psum(jnp.where(mine, array, jnp.zeros_like(array)), axis)


def shifted(block, axis, distance):
    devices = range(lax.axis_size(axis))
    route = [(i - distance, i) for i in devices if i - distance in devices]
    return lax.ppermute(block, axis, route)


def slot_table(query_blocks, kept_rows, sink_count, window_count):
    current = query_blocks[:, None]
    number = query_blocks.shape[0]
    sink_ids = jnp.broadcast_to(
        jnp.arange(SINK_MOST, dtype=jnp.int32)[None, :], (number, SINK_MOST)
    )
    sink_ok = (sink_ids < sink_count) & (sink_ids <= current) & (current - sink_ids >= window_count)
    offsets = jnp.arange(WIN_MOST, dtype=jnp.int32)[None, :]
    window_ids = current - offsets
    window_ok = (offsets < window_count) & (window_ids >= 0)
    kept_ok = (
        (kept_rows <= current) & (kept_rows >= sink_count) & (current - kept_rows >= window_count)
    )
    repeated = jnp.zeros((number,), dtype=bool)
    fresh = [jnp.logical_not(repeated)]
    kept_ok = kept_ok & jnp.stack(fresh, axis=1)
    slot_ids = jnp.concatenate([sink_ids, window_ids, kept_rows], axis=1)
    slot_ok = jnp.concatenate([sink_ok, window_ok, kept_ok], axis=1)
    return (jnp.maximum(slot_ids, 0), slot_ok)


def slot_mask(slot_ok):
    number, slots = slot_ok.shape
    within = jnp.arange(BLK, dtype=jnp.int32)
    diagonal = within[None, :] <= within[:, None]
    on_diagonal = jnp.arange(slots, dtype=jnp.int32) == SINK_MOST
    allowed = slot_ok[:, None, :, None] & (
        jnp.logical_not(on_diagonal)[None, None, :, None] | diagonal[None, :, None, :]
    )
    return allowed.reshape(number, BLK, slots * BLK)


def body(queries, keys, values, out_grad, kept_blocks, sink_blocks, window_blocks):
    head_count = lax.axis_size("head")
    seq_count = lax.axis_size("seq")
    seq_index = lax.axis_index("seq")
    head_index = lax.axis_index("head")
    kv_total = keys.shape[1]
    repeat = head_count // kv_total
    keys_wide = jnp.repeat(keys, repeat, axis=1)
    values_wide = jnp.repeat(values, repeat, axis=1)
    q_local, k_local, v_local, grad_local = (
        lax.all_to_all(queries, "head", split_axis=1, concat_axis=0, tiled=True),
        lax.all_to_all(keys_wide, "head", split_axis=1, concat_axis=0, tiled=True),
        lax.all_to_all(values_wide, "head", split_axis=1, concat_axis=0, tiled=True),
        lax.all_to_all(out_grad, "head", split_axis=1, concat_axis=0, tiled=True),
    )
    seq_rows, heads_here, width = q_local.shape
    local_blocks = seq_rows // BLK
    scale = 1.0 / math.sqrt(width)
    kv_pairs = jnp.concatenate([k_local[:, 0], v_local[:, 0]], axis=1)
    pair_blocks = kv_pairs.reshape(local_blocks, BLK, 2 * width)
    sink_pairs = spread(kv_pairs[: SINK_MOST * BLK], "seq", 0).reshape(SINK_MOST, BLK, 2 * width)
    reach = WIN_MOST - 1
    before = shifted(kv_pairs[seq_rows - reach * BLK :], "seq", 1)
    extended = jnp.concatenate([before, kv_pairs], axis=0).reshape(
        local_blocks + reach, BLK, 2 * width
    )
    kv_head = head_index // repeat
    head_lists = lax.dynamic_index_in_dim(kept_blocks, kv_head, 0, keepdims=False)
    sink_count = lax.dynamic_index_in_dim(sink_blocks, kv_head, 0, keepdims=False)
    window_count = lax.dynamic_index_in_dim(window_blocks, kv_head, 0, keepdims=False)
    keep = head_lists.shape[1]
    entries = local_blocks * keep
    capacity = max(2, -(-entries // seq_count))
    all_lists = head_lists.reshape(seq_count, entries)
    owners = all_lists // local_blocks
    order = jnp.arange(entries, dtype=jnp.int32)
    earlier_mask = order[None, :] < order[:, None]
    ranks = jnp.sum(
        ((owners[:, :, None] == owners[:, None, :]) & earlier_mask[None]).astype(jnp.int32), axis=2
    )
    place_ids = jnp.arange(capacity, dtype=jnp.int32)
    sent_match = (owners[:, None, :] == seq_index) & (ranks[:, None, :] == place_ids[None, :, None])
    sent_block = jnp.sum(
        jnp.where(sent_match, all_lists[:, None, :] - seq_index * local_blocks, 0), axis=2
    )
    outgoing = pair_blocks[sent_block]
    incoming = lax.all_to_all(outgoing, "seq", split_axis=0, concat_axis=0, tiled=True)
    my_lists = lax.dynamic_index_in_dim(all_lists, seq_index, 0, keepdims=False)
    my_owners = my_lists // local_blocks
    my_ranks = lax.dynamic_index_in_dim(ranks, seq_index, 0, keepdims=False)
    far_pairs = incoming.reshape(seq_count * capacity, BLK, 2 * width)[
        my_owners * capacity + my_ranks
    ]
    query_blocks = seq_index * local_blocks + jnp.arange(local_blocks, dtype=jnp.int32)
    unused_ids, slot_ok = slot_table(
        query_blocks, my_lists.reshape(local_blocks, keep), sink_count, window_count
    )
    allowed = slot_mask(slot_ok)
    slots = SINK_MOST + WIN_MOST + keep
    span = 2
    turns = local_blocks // span
    window_index = np.array(
        [[row + reach - offset for offset in range(WIN_MOST)] for row in range(span)],
        dtype=np.int32,
    )

    def turn(carry, inputs):
        near_sum, sink_sum = carry
        position, q_part, g_part, mask_part, far_part = inputs
        window_part = lax.dynamic_slice_in_dim(extended, position * span, span + reach, 0)
        window_slots = window_part[window_index]
        sink_slots = jnp.broadcast_to(sink_pairs[None], (span,) + sink_pairs.shape)
        gathered = jnp.concatenate([sink_slots, window_slots, far_part], axis=1).reshape(
            span, slots * BLK, 2 * width
        )
        key_part = gathered[..., :width]
        value_part = gathered[..., width:]
        scores = (
            jnp.einsum("bthd,bud->bhtu", q_part, key_part, preferred_element_type=jnp.float32)
            * scale
        )
        scores = jnp.where(mask_part[:, None], scores, -jnp.inf)
        top = jnp.max(scores, axis=3, keepdims=True)
        lse = top + jnp.log(jnp.sum(jnp.exp(scores - top), axis=3, keepdims=True))
        probs = jnp.exp(scores - lse)
        probs_low = probs.astype(jnp.bfloat16)
        dprobs = jnp.einsum(
            "bthd,bud->bhtu", g_part, value_part, preferred_element_type=jnp.float32
        )
        delta = jnp.sum(probs * dprobs, axis=3, keepdims=True)
        dscores = (probs * (dprobs - delta)).astype(jnp.bfloat16)
        grad_q = (
            jnp.einsum("bhtu,bud->bthd", dscores, key_part, preferred_element_type=jnp.float32)
            * scale
        ).astype(jnp.bfloat16)
        key_terms = (
            jnp.einsum("bhtu,bthd->bud", dscores, q_part, preferred_element_type=jnp.float32)
            * scale
        )
        value_terms = jnp.einsum(
            "bhtu,bthd->bud", probs_low, g_part, preferred_element_type=jnp.float32
        )
        terms = jnp.concatenate([key_terms, value_terms], axis=2).reshape(
            span, slots, BLK, 2 * width
        )
        sink_sum = sink_sum + jnp.sum(terms[:, :SINK_MOST], axis=0)
        window_terms = terms[:, SINK_MOST : SINK_MOST + WIN_MOST]
        placed = (
            jnp.zeros((span + reach, BLK, 2 * width), jnp.float32)
            .at[window_index]
            .add(window_terms)
        )
        previous = lax.dynamic_slice_in_dim(near_sum, position * span, span + reach, 0)
        near_sum = lax.dynamic_update_slice_in_dim(near_sum, previous + placed, position * span, 0)
        return ((near_sum, sink_sum), (grad_q, terms[:, SINK_MOST + WIN_MOST :]))

    start = (
        jnp.zeros((local_blocks + reach, BLK, 2 * width), jnp.float32),
        jnp.zeros((SINK_MOST, BLK, 2 * width), jnp.float32),
    )
    scan_inputs = (
        jnp.arange(turns, dtype=jnp.int32),
        q_local.reshape(turns, span, BLK, heads_here, width),
        grad_local.reshape(turns, span, BLK, heads_here, width),
        allowed.reshape(turns, span, BLK, slots * BLK),
        far_pairs.reshape(turns, span, keep, BLK, 2 * width),
    )
    (near_sum, sink_sum), (grad_blocks, far_terms) = lax.scan(turn, start, scan_inputs)
    grad_rows = grad_blocks.reshape(seq_rows, heads_here, width)
    grad_queries = lax.all_to_all(grad_rows, "head", split_axis=0, concat_axis=1, tiled=True)
    far_terms = far_terms.reshape(entries, BLK, 2 * width)
    owner_ids = jnp.arange(seq_count, dtype=jnp.int32)
    back_match = (my_owners[None, None, :] == owner_ids[:, None, None]) & (
        my_ranks[None, None, :] == place_ids[None, :, None]
    )
    outbound = jnp.einsum(
        "ocp,pbd->ocbd", back_match.astype(jnp.float32), far_terms, precision=lax.Precision.HIGHEST
    )
    sent_valid = jnp.any(sent_match, axis=2)
    owner_hits = (
        (sent_block[:, :, None] == jnp.arange(local_blocks, dtype=jnp.int32)[None, None, :])
        & sent_valid[:, :, None]
    ).astype(jnp.float32)
    arrived = lax.all_to_all(outbound, "seq", split_axis=0, concat_axis=0, tiled=True)
    far_added = jnp.einsum("rcb,rctd->btd", owner_hits, arrived, precision=lax.Precision.HIGHEST)
    spill = shifted(near_sum[:reach], "seq", -1)
    sink_total = lax.psum(sink_sum, "seq")
    own = near_sum[reach:] + far_added
    own = own + jnp.concatenate(
        [jnp.zeros((local_blocks - reach, BLK, 2 * width), jnp.float32), spill], axis=0
    )
    sink_share = jnp.where(seq_index == 0, sink_total, jnp.zeros_like(sink_total))
    own = own + jnp.concatenate(
        [sink_share, jnp.zeros((local_blocks - SINK_MOST, BLK, 2 * width), jnp.float32)], axis=0
    )
    flat = own.reshape(seq_rows, 1, 2 * width)
    returned = lax.all_to_all(flat, "head", split_axis=0, concat_axis=1, tiled=True)
    tok_rows = returned.shape[0]
    combined = jnp.sum(returned.reshape(tok_rows, kv_total, repeat, 2 * width), axis=2)
    grad_keys = combined[..., :width].astype(jnp.bfloat16)
    grad_values = combined[..., width:].astype(jnp.bfloat16)
    return (grad_queries, grad_keys, grad_values)


def solution(mesh):
    placed = (
        P(("dp", "seq", "head"), None, None),
        P(("dp", "seq", "head"), None, None),
        P(("dp", "seq", "head"), None, None),
        P(("dp", "seq", "head"), None, None),
        P(),
        P(),
        P(),
    )
    return jax.shard_map(
        body,
        mesh=mesh,
        in_specs=placed,
        out_specs=(
            P(("dp", "seq", "head"), None, None),
            P(("dp", "seq", "head"), None, None),
            P(("dp", "seq", "head"), None, None),
        ),
        check_vma=False,
    )
```

profile of v0, /device:TPU:32, one launch (start us, length us, event | category | flops | bytes accessed | tf_op | source)
XLA Modules:
  0.0 896.1 jit_solution(6246537948425911620)
XLA Ops:
  9.0 15.2 %all-to-all-start = ((bf16[128,16,128]{2,0,1:T(8,128)(2,1)}), bf16[128,16,128]{2,0,1:T(8,128)(2,1)S(1)}, u32[]{:S(2)}, u32[]{:S(2)}) async-start(bf16[128,16,128]{2,0,1:T(8,128)(2,1)} %bitcast.5), calls=%async_computation | async-start | bytes 1048576 | tf_op jit(solution)/shard_map/all_to_all | solution.py:67
  25.1 27.3 %all-to-all-done = bf16[128,16,128]{2,0,1:T(8,128)(2,1)S(1)} async-done(((bf16[128,16,128]{2,0,1:T(8,128)(2,1)}), bf16[128,16,128]{2,0,1:T(8,128)(2,1)S(1)}, u32[]{:S(2)}, u32[]{:S(2)}) %all-to-all-start) | async-done | bytes 524320 | tf_op jit(solution)/shard_map/all_to_all | solution.py:67
  53.4 7.2 all-to-all-start.1
  61.4 27.4 %all-to-all-done.1 = bf16[128,16,128]{2,0,1:T(8,128)(2,1)S(1)} async-done(((bf16[128,16,128]{2,0,1:T(8,128)(2,1)}), bf16[128,16,128]{2,0,1:T(8,128)(2,1)S(1)}, u32[]{:S(2)}, u32[]{:S(2)}) %all-to-all-start.1) | async-done | bytes 524320 | tf_op jit(solution)/shard_map/all_to_all | solution.py:68
  91.0 7.2 all-to-all-start.2
  99.6 25.4 %all-to-all-done.2 = bf16[16,2,128,256]{3,2,1,0:T(8,128)(2,1)} async-done(((bf16[16,2,128,256]{3,2,1,0:T(8,128)(2,1)}), bf16[16,2,128,256]{3,2,1,0:T(8,128)(2,1)}, u32[]{:S(2)}, u32[]{:S(2)}) %all-to-all-start.2) | async-done | bytes 2097184 | tf_op jit(solution)/shard_map/all_to_all | solution.py:102
  125.0 12.1 %all-to-all-start.3 = ((bf16[128,32,128]{2,0,1:T(8,128)(2,1)}), bf16[128,32,128]{2,0,1:T(8,128)(2,1)}, u32[]{:S(2)}, u32[]{:S(2)}) async-start(bf16[128,32,128]{2,0,1:T(8,128)(2,1)} %copy.112), calls=%async_computation.3 | async-start | bytes 2097152 | tf_op jit(solution)/shard_map/all_to_all | solution.py:66
  138.6 45.9 %all-to-all-done.3 = bf16[128,32,128]{2,0,1:T(8,128)(2,1)} async-done(((bf16[128,32,128]{2,0,1:T(8,128)(2,1)}), bf16[128,32,128]{2,0,1:T(8,128)(2,1)}, u32[]{:S(2)}, u32[]{:S(2)}) %all-to-all-start.3) | async-done | bytes 1048608 | tf_op jit(solution)/shard_map/all_to_all | solution.py:66
  184.5 9.5 %all-to-all-start.4 = ((bf16[128,32,128]{2,0,1:T(8,128)(2,1)}), bf16[128,32,128]{2,0,1:T(8,128)(2,1)}, u32[]{:S(2)}, u32[]{:S(2)}) async-start(bf16[128,32,128]{2,0,1:T(8,128)(2,1)} %copy.113), calls=%async_computation.4 | async-start | bytes 2097152 | tf_op jit(solution)/shard_map/all_to_all | solution.py:69
  200.1 4.7 broadcast_and_fusion
  214.2 108.9 %all-reduce.5.cloned.1.call-done = bf16[384,256]{1,0:T(8,128)(2,1)} async-done(((bf16[384,256]{1,0:T(8,128)(2,1)}), bf16[384,256]{1,0:T(8,128)(2,1)}) %all-reduce.5.cloned.1.call-update) | async-done | bytes 196624 | tf_op jit(solution)/shard_map/psum | solution.py:15
  324.8 233.6 %while.19 = (s32[]{:T(128)}, f32[19,128,256]{2,1,0:T(8,128)}, f32[3,128,256]{1,0,2:T(4,128)}, bf16[8,2,128,2,128]{4,2,1,0,3:T(8,128)(2,1)}, f32[8,2,1,128,256]{3...) while((s32[]{:T(128)}, f32[19,128,256]{2,1,0:T(8,128)}, ...), condition=%wide.region_9.10_spmd.clone.clone.clone, body=%wide.region_3.9_spmd.sunk.clone.clone.clone.sunk | while | flops 680951808 | bytes 64059104 | solution.py:183
  341.9 3.7 scatter_fusion
  370.9 3.7 scatter_fusion
  562.5 5.3 copy.120
  567.8 5.2 all-to-all-start.6
  573.0 9.5 %copy.115 = bf16[2048,2,128]{2,1,0:T(2,128)(2,1)} copy(bf16[2048,2,128]{2,0,1:T(8,128)(2,1)S(1)} %bitcast.244) | data formatting | bytes 2097152 | tf_op jit(solution)/shard_map/reshape | solution.py:184
  582.5 50.3 %all-to-all-done.6 = f32[16,2,128,256]{3,1,2,0:T(2,128)} async-done(((f32[16,2,128,256]{3,1,2,0:T(2,128)}), f32[16,2,128,256]{3,1,2,0:T(2,128)}, u32[]{:S(2)}, u32[]{:S(2)}) %all-to-all-start.6) | async-done | bytes 4194336 | tf_op jit(solution)/shard_map/all_to_all | solution.py:199
  632.8 12.7 %all-to-all-start.5 = ((bf16[2048,2,128]{2,1,0:T(2,128)(2,1)}), bf16[2048,2,128]{2,1,0:T(2,128)(2,1)}, u32[]{:S(2)}, u32[]{:S(2)}) async-start(bf16[2048,2,128]{2,1,0:T(2,128)(2,1)} %copy.115), calls=%async_computation.5 | async-start | bytes 2097152 | tf_op jit(solution)/shard_map/all_to_all | solution.py:185
  651.5 111.6 %all-reduce.7.cloned.1.call-done = f32[3,128,256]{2,0,1:T(4,128)} async-done(((f32[3,128,256]{2,0,1:T(4,128)}), f32[3,128,256]{2,0,1:T(4,128)}) %all-reduce.7.cloned.1.call-update) | async-done | bytes 393232 | tf_op jit(solution)/shard_map/psum | solution.py:202
  764.3 7.5 fusion.25
  773.0 10.0 %copy.125 = f32[2048,1,256]{2,1,0:T(1,128)} copy(f32[2048,1,256]{2,0,1:T(8,128)S(1)} %bitcast.231) | data formatting | bytes 4194304 | tf_op jit(solution)/shard_map/reshape | solution.py:211
  783.0 12.7 %all-to-all-start.7 = ((f32[2048,1,256]{2,1,0:T(1,128)}), f32[2048,1,256]{2,1,0:T(1,128)S(1)}, u32[]{:S(2)}, u32[]{:S(2)}) async-start(f32[2048,1,256]{2,1,0:T(1,128)} %copy.125), calls=%async_computation.7 | async-start | bytes 4194304 | tf_op jit(solution)/shard_map/all_to_all | solution.py:212
  798.8 88.6 %all-to-all-done.7 = f32[2048,1,256]{2,1,0:T(1,128)S(1)} async-done(((f32[2048,1,256]{2,1,0:T(1,128)}), f32[2048,1,256]{2,1,0:T(1,128)S(1)}, u32[]{:S(2)}, u32[]{:S(2)}) %all-to-all-start.7) | async-done | bytes 2097184 | tf_op jit(solution)/shard_map/all_to_all | solution.py:212
  (420 shorter events, 263.9 us)
Async XLA Ops:
  7.2 53.4 %copy-start = (s32[4,256,1]{1,2,0:T(1,128)S(1)}, s32[4,256,1]{1,2,0:T(1,128)}, u32[]{:S(2)}) copy-start(s32[4,256,1]{1,2,0:T(1,128)} %param.16) | copy-start | bytes 12292
  9.0 43.4 %all-to-all-start = ((bf16[128,16,128]{2,0,1:T(8,128)(2,1)}), bf16[128,16,128]{2,0,1:T(8,128)(2,1)S(1)}, u32[]{:S(2)}, u32[]{:S(2)}) async-start(bf16[128,16,128]{2,0,1:T(8,128)(2,1)} %bitcast.5), calls=%async_computation | async-start | bytes 1048576 | tf_op jit(solution)/shard_map/all_to_all | solution.py:67
  53.4 35.4 %all-to-all-start.1 = ((bf16[128,16,128]{2,0,1:T(8,128)(2,1)}), bf16[128,16,128]{2,0,1:T(8,128)(2,1)S(1)}, u32[]{:S(2)}, u32[]{:S(2)}) async-start(bf16[128,16,128]{2,0,1:T(8,128)(2,1)} %bitcast.9), calls=%async_computation.1 | async-start | bytes 1048576 | tf_op jit(solution)/shard_map/all_to_all | solution.py:68
  61.2 29.7 %copy-start.15 = (s32[16,2]{0,1:T(2,128)}, s32[16,2]{0,1:T(2,128)S(1)}, u32[]{:S(2)}) copy-start(s32[16,2]{0,1:T(2,128)S(1)} %select_reduce_fusion) | copy-start | bytes 388
  91.0 7.2 copy-start.9
  91.0 34.1 %all-to-all-start.2 = ((bf16[16,2,128,256]{3,2,1,0:T(8,128)(2,1)}), bf16[16,2,128,256]{3,2,1,0:T(8,128)(2,1)}, u32[]{:S(2)}, u32[]{:S(2)}) async-start(bf16[16,2,128,256]{3,2,1,0:T(8,128)(2,1)} %bitcast.19), calls=%async_computation.2 | async-start | bytes 4194304 | tf_op jit(solution)/shard_map/all_to_all | solution.py:102
  98.2 39.0 %copy-start.10 = (bf16[128,32,128]{2,1,0:T(8,128)(2,1)S(1)}, bf16[128,32,128]{2,1,0:T(8,128)(2,1)}, u32[]{:S(2)}) copy-start(bf16[128,32,128]{2,1,0:T(8,128)(2,1)} %param.15) | copy-start | bytes 3145732
  125.0 59.5 %all-to-all-start.3 = ((bf16[128,32,128]{2,0,1:T(8,128)(2,1)}), bf16[128,32,128]{2,0,1:T(8,128)(2,1)}, u32[]{:S(2)}, u32[]{:S(2)}) async-start(bf16[128,32,128]{2,0,1:T(8,128)(2,1)} %copy.112), calls=%async_computation.3 | async-start | bytes 2097152 | tf_op jit(solution)/shard_map/all_to_all | solution.py:66
  137.2 56.9 %copy-start.19 = (s32[4]{0:T(128)S(1)}, s32[4]{0:T(128)}, u32[]{:S(2)}) copy-start(s32[4]{0:T(128)} %param.17) | copy-start | bytes 52
  137.2 57.6 %copy-start.20 = (s32[4]{0:T(128)S(1)}, s32[4]{0:T(128)}, u32[]{:S(2)}) copy-start(s32[4]{0:T(128)} %param.18) | copy-start | bytes 52
  184.5 138.6 %all-to-all-start.4 = ((bf16[128,32,128]{2,0,1:T(8,128)(2,1)}), bf16[128,32,128]{2,0,1:T(8,128)(2,1)}, u32[]{:S(2)}, u32[]{:S(2)}) async-start(bf16[128,32,128]{2,0,1:T(8,128)(2,1)} %copy.113), calls=%async_computation.4 | async-start | bytes 2097152 | tf_op jit(solution)/shard_map/all_to_all | solution.py:69
  194.0 129.0 %all-reduce.5.cloned.1.call-start = ((), (), s32[]{:S(2)}) async-start(), calls=%async_computation.8 | async-start | bytes 393216 | tf_op jit(solution)/shard_map/psum | solution.py:15
  205.5 5.3 collective-permute-start
  211.0 113.9 %copy-start.12 = (s32[8]{0:T(128)S(1)}, s32[8]{0:T(128)}, u32[]{:S(2)}) copy-start(s32[8]{0:T(128)} %constant.226) | copy-start | bytes 100
  567.8 5.2 copy-start.11
  567.8 65.0 %all-to-all-start.6 = ((f32[16,2,128,256]{3,1,2,0:T(2,128)}), f32[16,2,128,256]{3,1,2,0:T(2,128)}, u32[]{:S(2)}, u32[]{:S(2)}) async-start(f32[16,2,128,256]{3,1,2,0:T(2,128)} %copy.120), calls=%async_computation.6 | async-start | bytes 8388608 | tf_op jit(solution)/shard_map/all_to_all | solution.py:199
  573.0 72.5 %copy-start.4 = (f32[3,128,256]{1,0,2:T(4,128)S(1)}, f32[3,128,256]{1,0,2:T(4,128)}, u32[]{:S(2)}) copy-start(f32[3,128,256]{1,0,2:T(4,128)} %get-tuple-element.86) | copy-start | bytes 1179652
  582.5 64.1 %copy-start.3 = (f32[19,128,256]{2,1,0:T(8,128)S(1)}, f32[19,128,256]{2,1,0:T(8,128)}, u32[]{:S(2)}) copy-start(f32[19,128,256]{2,1,0:T(8,128)} %get-tuple-element.84) | copy-start | bytes 7471108
  632.8 150.2 %all-to-all-start.5 = ((bf16[2048,2,128]{2,1,0:T(2,128)(2,1)}), bf16[2048,2,128]{2,1,0:T(2,128)(2,1)}, u32[]{:S(2)}, u32[]{:S(2)}) async-start(bf16[2048,2,128]{2,1,0:T(2,128)(2,1)} %copy.115), calls=%async_computation.5 | async-start | bytes 2097152 | tf_op jit(solution)/shard_map/all_to_all | solution.py:185
  645.5 117.7 %all-reduce.7.cloned.1.call-start = ((), (), s32[]{:S(2)}) async-start(), calls=%async_computation.9 | async-start | bytes 1048576 | tf_op jit(solution)/shard_map/psum | solution.py:202
  646.6 4.8 copy-start.14
  649.7 114.6 %copy-start.16 = (s32[16,2]{0,1:T(2,128)S(1)}, s32[16,2]{0,1:T(2,128)}, u32[]{:S(2)}) copy-start(s32[16,2]{0,1:T(2,128)} %copy-done.15) | copy-start | bytes 388
  649.8 114.5 %collective-permute-start.1 = (f32[3,128,256]{2,0,1:T(4,128)S(1)}, f32[3,128,256]{2,0,1:T(4,128)S(1)}, u32[]{:S(2)}, u32[]{:S(2)}) collective-permute-start(f32[3,128,256]{2,0,1:T(4,128)S(1)} %slice.73), channel_id=1, source_target_pairs={{16,0},{32,16},{48,32},{64,48},{80,64},{96,80},{112,96},{128,112},... | collective-permute-start | bytes 1179656 | tf_op jit(solution)/shard_map/ppermute | solution.py:21
  783.0 104.4 %all-to-all-start.7 = ((f32[2048,1,256]{2,1,0:T(1,128)}), f32[2048,1,256]{2,1,0:T(1,128)S(1)}, u32[]{:S(2)}, u32[]{:S(2)}) async-start(f32[2048,1,256]{2,1,0:T(1,128)} %copy.125), calls=%async_computation.7 | async-start | bytes 4194304 | tf_op jit(solution)/shard_map/all_to_all | solution.py:212
  (46 other events, 140.9 us)
Sparse Core Ops, SparseCore 0:
  207.7 115.3 all-reduce.4
  649.5 113.5 all-reduce.6
where the time goes:
time: 900 us; the launch traced here: 896 us
  waiting for transfers between devices  489 us (54%)
  local copies, waits for them, and re-layouts  160 us (18%)
  starting transfers between devices  84.9 us (9%)
  other arithmetic  76.4 us (8%)
  matrix products  65 us (7%)
  between operations  14.5 us (2%)
    psum x1, waiting for transfers between devices, body(): sink_total = lax.psum(sink_sum, 'seq')  112 us
    psum x1, waiting for transfers between devices, spread(): return lax.psum(jnp.where(mine, array, jnp.zeros_like(array)), axis)  109 us
    all_to_all x1, waiting for transfers between devices, body(): lax.all_to_all(flat, 'head', split_axis=0, concat_axis=1, tiled=True)  88.6 us
    all_to_all x1, waiting for transfers between devices, body(): lax.all_to_all(outbound, 'seq', split_axis=0, concat_axis=0, tiled=True)  50.3 us
    all_to_all x1, waiting for transfers between devices, body(): lax.all_to_all(queries, 'head', split_axis=1, concat_axis=0, tiled=True)  45.9 us
    slice x16, local copies, waits for them, and re-layouts, turn(): window_terms = terms[:, SINK_MOST:SINK_MOST + WIN_MOST]  29.9 us
    scatter-add x8, other arithmetic, turn(): placed = jnp.zeros((span + reach, BLK, 2 * width), jnp.float32).at[window...  29.2 us
    all_to_all x1, waiting for transfers between devices, body(): lax.all_to_all(values_wide, 'head', split_axis=1, concat_axis=0, tiled=True)  27.4 us
  transfers between devices with their start and end apart: 12, of which 9 were waited for; matrix products, arithmetic and copies ran while one was open for 6% of the time, Pallas kernels for 0%

commit v1 on v0

--- a/solution.py
+++ b/solution.py
@@ -199,7 +199,7 @@
     arrived = lax.all_to_all(outbound, "seq", split_axis=0, concat_axis=0, tiled=True)
     far_added = jnp.einsum("rcb,rctd->btd", owner_hits, arrived, precision=lax.Precision.HIGHEST)
     spill = shifted(near_sum[:reach], "seq", -1)
-    sink_total = lax.psum(sink_sum, "seq")
+    sink_total = lax.all_gather(sink_sum, "seq").sum(axis=0)
     own = near_sum[reach:] + far_added
     own = own + jnp.concatenate(
         [jnp.zeros((local_blocks - reach, BLK, 2 * width), jnp.float32), spill], axis=0

time: 900 us -> 823 us (0.914)
  the two profiles are of different devices: /device:TPU:32 before, /device:TPU:2 now
where the time goes in v1:
time: 823 us; the launch traced here: 819 us
  waiting for transfers between devices  402 us (49%)
  local copies, waits for them, and re-layouts  163 us (20%)
  starting transfers between devices  92.7 us (11%)
  other arithmetic  77 us (9%)
  matrix products  64.2 us (8%)
  between operations  14.6 us (2%)
    psum x1, waiting for transfers between devices, spread(): return lax.psum(jnp.where(mine, array, jnp.zeros_like(array)), axis)  107 us
    all_to_all x1, waiting for transfers between devices, body(): lax.all_to_all(flat, 'head', split_axis=0, concat_axis=1, tiled=True)  92.5 us
    all_to_all x1, waiting for transfers between devices, body(): lax.all_to_all(queries, 'head', split_axis=1, concat_axis=0, tiled=True)  48 us
    all_to_all x1, waiting for transfers between devices, body(): lax.all_to_all(outbound, 'seq', split_axis=0, concat_axis=0, tiled=True)  47.9 us
    slice x16, local copies, waits for them, and re-layouts, turn(): window_terms = terms[:, SINK_MOST:SINK_MOST + WIN_MOST]  30.2 us
    scatter-add x8, other arithmetic, turn(): placed = jnp.zeros((span + reach, BLK, 2 * width), jnp.float32).at[window...  28.9 us
    all_to_all x1, waiting for transfers between devices, body(): lax.all_to_all(values_wide, 'head', split_axis=1, concat_axis=0, tiled=True)  28.2 us
    all_to_all x1, waiting for transfers between devices, body(): lax.all_to_all(keys_wide, 'head', split_axis=1, concat_axis=0, tiled=True)  28.2 us
  transfers between devices with their start and end apart: 12, of which 9 were waited for; matrix products, arithmetic and copies ran while one was open for 8% of the time, Pallas kernels for 0%

profile of v1, /device:TPU:2, one launch (start us, length us, event | category | flops | bytes accessed | tf_op | source)
XLA Modules:
  0.0 819.3 jit_solution(1408217737567059735)
XLA Ops:
  9.0 15.2 %all-to-all-start = ((bf16[128,16,128]{2,0,1:T(8,128)(2,1)}), bf16[128,16,128]{2,0,1:T(8,128)(2,1)S(1)}, u32[]{:S(2)}, u32[]{:S(2)}) async-start(bf16[128,16,128]{2,0,1:T(8,128)(2,1)} %bitcast.5), calls=%async_computation | async-start | bytes 1048576 | tf_op jit(solution)/shard_map/all_to_all | solution.py:67
  25.1 28.2 %all-to-all-done = bf16[128,16,128]{2,0,1:T(8,128)(2,1)S(1)} async-done(((bf16[128,16,128]{2,0,1:T(8,128)(2,1)}), bf16[128,16,128]{2,0,1:T(8,128)(2,1)S(1)}, u32[]{:S(2)}, u32[]{:S(2)}) %all-to-all-start) | async-done | bytes 524320 | tf_op jit(solution)/shard_map/all_to_all | solution.py:67
  54.2 6.3 all-to-all-start.1
  61.4 28.2 %all-to-all-done.1 = bf16[128,16,128]{2,0,1:T(8,128)(2,1)S(1)} async-done(((bf16[128,16,128]{2,0,1:T(8,128)(2,1)}), bf16[128,16,128]{2,0,1:T(8,128)(2,1)S(1)}, u32[]{:S(2)}, u32[]{:S(2)}) %all-to-all-start.1) | async-done | bytes 524320 | tf_op jit(solution)/shard_map/all_to_all | solution.py:68
  91.8 7.6 all-to-all-start.2
  100.8 21.8 %all-to-all-done.2 = bf16[16,2,128,256]{3,2,1,0:T(8,128)(2,1)} async-done(((bf16[16,2,128,256]{3,2,1,0:T(8,128)(2,1)}), bf16[16,2,128,256]{3,2,1,0:T(8,128)(2,1)}, u32[]{:S(2)}, u32[]{:S(2)}) %all-to-all-start.2) | async-done | bytes 2097184 | tf_op jit(solution)/shard_map/all_to_all | solution.py:102
  122.6 10.4 %all-to-all-start.3 = ((bf16[128,32,128]{2,0,1:T(8,128)(2,1)}), bf16[128,32,128]{2,0,1:T(8,128)(2,1)}, u32[]{:S(2)}, u32[]{:S(2)}) async-start(bf16[128,32,128]{2,0,1:T(8,128)(2,1)} %copy.110), calls=%async_computation.3 | async-start | bytes 2097152 | tf_op jit(solution)/shard_map/all_to_all | solution.py:66
  134.5 48.0 %all-to-all-done.3 = bf16[128,32,128]{2,0,1:T(8,128)(2,1)} async-done(((bf16[128,32,128]{2,0,1:T(8,128)(2,1)}), bf16[128,32,128]{2,0,1:T(8,128)(2,1)}, u32[]{:S(2)}, u32[]{:S(2)}) %all-to-all-start.3) | async-done | bytes 1048608 | tf_op jit(solution)/shard_map/all_to_all | solution.py:66
  182.4 8.0 all-to-all-start.4
  195.7 4.6 broadcast_and_fusion
  205.9 5.3 collective-permute-done
  214.6 106.8 %all-reduce.4.cloned.1.call-done = bf16[384,256]{1,0:T(8,128)(2,1)} async-done(((bf16[384,256]{1,0:T(8,128)(2,1)}), bf16[384,256]{1,0:T(8,128)(2,1)}) %all-reduce.4.cloned.1.call-update) | async-done | bytes 196624 | tf_op jit(solution)/shard_map/psum | solution.py:15
  323.2 232.7 %while.19 = (s32[]{:T(128)}, f32[19,128,256]{2,1,0:T(8,128)}, f32[3,128,256]{1,0,2:T(4,128)}, bf16[8,2,128,2,128]{4,2,1,0,3:T(8,128)(2,1)}, f32[8,2,1,128,256]{3...) while((s32[]{:T(128)}, f32[19,128,256]{2,1,0:T(8,128)}, ...), condition=%wide.region_9.10_spmd.clone.clone.clone, body=%wide.region_3.9_spmd.sunk.clone.clone.clone.sunk | while | flops 680951808 | bytes 64059104 | solution.py:183
  562.6 5.3 copy.118
  567.9 6.1 all-to-all-start.6
  574.1 9.5 %copy.113 = bf16[2048,2,128]{2,1,0:T(2,128)(2,1)} copy(bf16[2048,2,128]{2,0,1:T(8,128)(2,1)S(1)} %bitcast.246) | data formatting | bytes 2097152 | tf_op jit(solution)/shard_map/reshape | solution.py:184
  583.5 47.9 %all-to-all-done.6 = f32[16,2,128,256]{3,1,2,0:T(2,128)} async-done(((f32[16,2,128,256]{3,1,2,0:T(2,128)}), f32[16,2,128,256]{3,1,2,0:T(2,128)}, u32[]{:S(2)}, u32[]{:S(2)}) %all-to-all-start.6) | async-done | bytes 4194336 | tf_op jit(solution)/shard_map/all_to_all | solution.py:199
  631.4 12.3 %all-to-all-start.5 = ((bf16[2048,2,128]{2,1,0:T(2,128)(2,1)}), bf16[2048,2,128]{2,1,0:T(2,128)(2,1)}, u32[]{:S(2)}, u32[]{:S(2)}) async-start(bf16[2048,2,128]{2,1,0:T(2,128)(2,1)} %copy.113), calls=%async_computation.5 | async-start | bytes 2097152 | tf_op jit(solution)/shard_map/all_to_all | solution.py:185
  648.0 9.6 %collective-permute-start.1 = (f32[3,128,256]{2,0,1:T(4,128)}, f32[3,128,256]{2,0,1:T(4,128)}, u32[]{:S(2)}, u32[]{:S(2)}) collective-permute-start(f32[3,128,256]{2,0,1:T(4,128)} %slice.73), channel_id=1, source_target_pairs={{16,0},{32,16},{48,32},{64,48},{80,64},{96,80},{112,96},{128,112},... | collective-permute-start | bytes 1179656 | tf_op jit(solution)/shard_map/ppermute | solution.py:21
  657.7 23.2 %all-gather.3.cloned.1.call-done = f32[48,128,256]{2,1,0:T(8,128)} async-done(((f32[3,128,256]{2,1,0:T(8,128)}), f32[48,128,256]{2,1,0:T(8,128)}) %all-gather.3.cloned.1.call-update) | async-done | bytes 6291472 | tf_op jit(solution)/shard_map/all_gather | solution.py:202
  684.7 6.7 fusion.25
  692.6 10.0 %copy.124 = f32[2048,1,256]{2,1,0:T(1,128)} copy(f32[2048,1,256]{2,0,1:T(8,128)S(1)} %bitcast.232) | data formatting | bytes 4194304 | tf_op jit(solution)/shard_map/reshape | solution.py:211
  702.6 12.3 %all-to-all-start.7 = ((f32[2048,1,256]{2,1,0:T(1,128)}), f32[2048,1,256]{2,1,0:T(1,128)S(1)}, u32[]{:S(2)}, u32[]{:S(2)}) async-start(f32[2048,1,256]{2,1,0:T(1,128)} %copy.124), calls=%async_computation.7 | async-start | bytes 4194304 | tf_op jit(solution)/shard_map/all_to_all | solution.py:212
  718.0 92.5 %all-to-all-done.7 = f32[2048,1,256]{2,1,0:T(1,128)S(1)} async-done(((f32[2048,1,256]{2,1,0:T(1,128)}), f32[2048,1,256]{2,1,0:T(1,128)S(1)}, u32[]{:S(2)}, u32[]{:S(2)}) %all-to-all-start.7) | async-done | bytes 2097184 | tf_op jit(solution)/shard_map/all_to_all | solution.py:212
  (421 shorter events, 272.6 us)
Async XLA Ops:
  7.2 53.4 %copy-start = (s32[4,256,1]{1,2,0:T(1,128)S(1)}, s32[4,256,1]{1,2,0:T(1,128)}, u32[]{:S(2)}) copy-start(s32[4,256,1]{1,2,0:T(1,128)} %param.16) | copy-start | bytes 12292
  9.0 44.3 %all-to-all-start = ((bf16[128,16,128]{2,0,1:T(8,128)(2,1)}), bf16[128,16,128]{2,0,1:T(8,128)(2,1)S(1)}, u32[]{:S(2)}, u32[]{:S(2)}) async-start(bf16[128,16,128]{2,0,1:T(8,128)(2,1)} %bitcast.5), calls=%async_computation | async-start | bytes 1048576 | tf_op jit(solution)/shard_map/all_to_all | solution.py:67
  54.2 35.4 %all-to-all-start.1 = ((bf16[128,16,128]{2,0,1:T(8,128)(2,1)}), bf16[128,16,128]{2,0,1:T(8,128)(2,1)S(1)}, u32[]{:S(2)}, u32[]{:S(2)}) async-start(bf16[128,16,128]{2,0,1:T(8,128)(2,1)} %bitcast.9), calls=%async_computation.1 | async-start | bytes 1048576 | tf_op jit(solution)/shard_map/all_to_all | solution.py:68
  61.1 144.5 %copy-start.13 = (s32[16,16]{1,0:T(8,128)}, s32[16,16]{1,0:T(8,128)S(1)}, u32[]{:S(2)}) copy-start(s32[16,16]{1,0:T(8,128)S(1)} %convert_reduce_fusion) | copy-start | bytes 3076
  61.2 30.5 %copy-start.17 = (s32[16,2]{0,1:T(2,128)}, s32[16,2]{0,1:T(2,128)S(1)}, u32[]{:S(2)}) copy-start(s32[16,2]{0,1:T(2,128)S(1)} %select_reduce_fusion) | copy-start | bytes 388
  91.8 7.6 copy-start.9
  91.8 30.8 %all-to-all-start.2 = ((bf16[16,2,128,256]{3,2,1,0:T(8,128)(2,1)}), bf16[16,2,128,256]{3,2,1,0:T(8,128)(2,1)}, u32[]{:S(2)}, u32[]{:S(2)}) async-start(bf16[16,2,128,256]{3,2,1,0:T(8,128)(2,1)} %bitcast.19), calls=%async_computation.2 | async-start | bytes 4194304 | tf_op jit(solution)/shard_map/all_to_all | solution.py:102
  99.4 33.6 %copy-start.10 = (bf16[128,32,128]{2,1,0:T(8,128)(2,1)S(1)}, bf16[128,32,128]{2,1,0:T(8,128)(2,1)}, u32[]{:S(2)}) copy-start(bf16[128,32,128]{2,1,0:T(8,128)(2,1)} %param.15) | copy-start | bytes 3145732
  122.6 59.8 %all-to-all-start.3 = ((bf16[128,32,128]{2,0,1:T(8,128)(2,1)}), bf16[128,32,128]{2,0,1:T(8,128)(2,1)}, u32[]{:S(2)}, u32[]{:S(2)}) async-start(bf16[128,32,128]{2,0,1:T(8,128)(2,1)} %copy.110), calls=%async_computation.3 | async-start | bytes 2097152 | tf_op jit(solution)/shard_map/all_to_all | solution.py:66
  133.0 57.5 %copy-start.19 = (s32[4]{0:T(128)S(1)}, s32[4]{0:T(128)}, u32[]{:S(2)}) copy-start(s32[4]{0:T(128)} %param.17) | copy-start | bytes 52
  133.1 58.1 %copy-start.20 = (s32[4]{0:T(128)S(1)}, s32[4]{0:T(128)}, u32[]{:S(2)}) copy-start(s32[4]{0:T(128)} %param.18) | copy-start | bytes 52
  182.4 139.0 %all-to-all-start.4 = ((bf16[128,32,128]{2,0,1:T(8,128)(2,1)}), bf16[128,32,128]{2,0,1:T(8,128)(2,1)}, u32[]{:S(2)}, u32[]{:S(2)}) async-start(bf16[128,32,128]{2,0,1:T(8,128)(2,1)} %copy.111), calls=%async_computation.4 | async-start | bytes 2097152 | tf_op jit(solution)/shard_map/all_to_all | solution.py:69
  190.5 131.0 %all-reduce.4.cloned.1.call-start = ((), (), s32[]{:S(2)}) async-start(), calls=%async_computation.8 | async-start | bytes 393216 | tf_op jit(solution)/shard_map/psum | solution.py:15
  201.0 10.2 %collective-permute-start = (bf16[384,256]{1,0:T(8,128)(2,1)S(1)}, bf16[384,256]{1,0:T(8,128)(2,1)S(1)}, u32[]{:S(2)}, u32[]{:S(2)}) collective-permute-start(bf16[384,256]{1,0:T(8,128)(2,1)S(1)} %get-tuple-element.239), channel_id=1, source_target_pairs={{0,16},{16,32},{32,48},{48,64},{64,80},{80,96},{96,112},{112,128},... | collective-permute-start | bytes 589832 | tf_op jit(solution)/shard_map/ppermute | solution.py:21
  205.7 475.2 %all-gather.3.cloned.1.call-start = ((), (), s32[]{:S(2)}) async-start(), calls=%async_computation.9 | async-start | bytes 6684672 | tf_op jit(solution)/shard_map/all_gather | solution.py:202
  211.4 111.8 %copy-start.12 = (s32[8]{0:T(128)S(1)}, s32[8]{0:T(128)}, u32[]{:S(2)}) copy-start(s32[8]{0:T(128)} %constant.226) | copy-start | bytes 100
  567.9 6.1 copy-start.11
  567.9 63.5 %all-to-all-start.6 = ((f32[16,2,128,256]{3,1,2,0:T(2,128)}), f32[16,2,128,256]{3,1,2,0:T(2,128)}, u32[]{:S(2)}, u32[]{:S(2)}) async-start(f32[16,2,128,256]{3,1,2,0:T(2,128)} %copy.118), calls=%async_computation.6 | async-start | bytes 8388608 | tf_op jit(solution)/shard_map/all_to_all | solution.py:199
  574.0 69.8 %copy-start.3 = (f32[19,128,256]{2,1,0:T(8,128)S(1)}, f32[19,128,256]{2,1,0:T(8,128)}, u32[]{:S(2)}) copy-start(f32[19,128,256]{2,1,0:T(8,128)} %get-tuple-element.84) | copy-start | bytes 7471108
  631.4 71.2 %all-to-all-start.5 = ((bf16[2048,2,128]{2,1,0:T(2,128)(2,1)}), bf16[2048,2,128]{2,1,0:T(2,128)(2,1)}, u32[]{:S(2)}, u32[]{:S(2)}) async-start(bf16[2048,2,128]{2,1,0:T(2,128)(2,1)} %copy.113), calls=%async_computation.5 | async-start | bytes 2097152 | tf_op jit(solution)/shard_map/all_to_all | solution.py:185
  643.8 13.8 %copy-start.14 = (s32[16,16]{1,0:T(8,128)S(1)}, s32[16,16]{1,0:T(8,128)}, u32[]{:S(2)}) copy-start(s32[16,16]{1,0:T(8,128)} %copy-done.13) | copy-start | bytes 3076
  643.8 13.8 %copy-start.16 = (pred[16,16]{1,0:T(8,128)(4,1)S(1)}, pred[16,16]{1,0:T(8,128)(4,1)}, u32[]{:S(2)}) copy-start(pred[16,16]{1,0:T(8,128)(4,1)} %copy-done.15) | copy-start | bytes 772
  648.0 36.7 %collective-permute-start.1 = (f32[3,128,256]{2,0,1:T(4,128)}, f32[3,128,256]{2,0,1:T(4,128)}, u32[]{:S(2)}, u32[]{:S(2)}) collective-permute-start(f32[3,128,256]{2,0,1:T(4,128)} %slice.73), channel_id=1, source_target_pairs={{16,0},{32,16},{48,32},{64,48},{80,64},{96,80},{112,96},{128,112},... | collective-permute-start | bytes 1179656 | tf_op jit(solution)/shard_map/ppermute | solution.py:21
  702.6 107.9 %all-to-all-start.7 = ((f32[2048,1,256]{2,1,0:T(1,128)}), f32[2048,1,256]{2,1,0:T(1,128)S(1)}, u32[]{:S(2)}, u32[]{:S(2)}) async-start(f32[2048,1,256]{2,1,0:T(1,128)} %copy.124), calls=%async_computation.7 | async-start | bytes 4194304 | tf_op jit(solution)/shard_map/all_to_all | solution.py:212
  (46 other events, 144.0 us)
Sparse Core Ops, SparseCore 0:
  205.8 115.5 all-reduce.3
  558.0 122.8 all-gather.2
